TPU v7x, 256 devices: a whole 4x4x8 slice. The times are simulated.
256 devices in a mesh: lon: 64 (over z, y_hi, x), lat: 4 (over y_lo, core).
Axes of the slice: x: 4, y: 4 (y_hi: 2, y_lo: 2; y = y_hi * 2 + y_lo), z: 8, core: 2. Of those that a mesh axis runs over, the one named last changes fastest.
Arguments:
- field: bfloat16 [2, 48, 1536, 192], P(None, 'lat', 'lon'), may hold values from -6 to 6
- region: int32 [48], replicated, may hold values from 0 to 2, never falling along the last dimension, each value on 1 to 24 neighbouring positions
- w_qkv: bfloat16 [192, 576], replicated, may hold values from -4 to 4
- w_out: bfloat16 [192, 192], replicated, may hold values from -0.4375 to 0.4375
- w_up: bfloat16 [192, 768], replicated, may hold values from -0.4375 to 0.4375
- w_down: bfloat16 [768, 192], replicated, may hold values from -0.21875 to 0.21875
- gain_attn: float32 [192], replicated, may hold values from 0.25 to 1.75
- gain_mlp: float32 [192], replicated, may hold values from 0.25 to 1.75
- grad_next: bfloat16 [2, 48, 1536, 192], P(None, 'lat', 'lon'), may hold values from -6 to 6
Outputs:
- output: bfloat16 [2, 48, 1536, 192], P(None, 'lat', 'lon')
- grad_field: bfloat16 [2, 48, 1536, 192], P(None, 'lat', 'lon')
- grad_qkv: float32 [192, 576], replicated
- grad_out: float32 [192, 192], replicated
- grad_up: float32 [192, 768], replicated
- grad_down: float32 [768, 192], replicated
- grad_gain_attn: float32 [192], replicated
- grad_gain_mlp: float32 [192], replicated
Inputs may be any that keep to these rules, and one draw needn't show every extreme that they name: `region`: bands never fall along latitude, each band is one run of rows, at most 24 rows.
All inputs are finite; a program needn't handle non-finite values.
Results may differ from a plain program's by a relative error of at most 0.015.
The roundings to bfloat16 on the way count: a program that leaves them out, or rounds other values in their place, can miss the bound.
Values may be sent and summed in bfloat16 or wider, within the bound.
A program may use at most 64 MiB of HBM per device.

v0:
```python
import functools

import jax
import jax.numpy as jnp
import ml_dtypes
import numpy as np
from jax import lax
from jax.experimental import pallas as pl
from jax.experimental.pallas import tpu as pltpu
from jax.sharding import PartitionSpec as P

C = 192
HEADS = 6
FF = 768
HALF = 384
ROWS = 12
COLS = 24
TOK = 2 * ROWS * COLS
SCALE = 32.0 ** -0.5
LOG2E = 1.4426950408889634
F32 = jnp.float32
BF = jnp.bfloat16
MESH = pl.DeviceIdType.MESH
VLIM = 54 << 20

NQ = (144,) + (72,) * 4 + (40,) * 4
NK = (144,) + (144,) * 4 + (160,) * 4
QAT = tuple(int(v) for v in np.cumsum((0,) + NQ))
KAT = tuple(int(v) for v in np.cumsum((0,) + NK))
NQS, NKS = QAT[-1], KAT[-1]
WAY = ((0, -1), (0, 1), (-1, 0), (1, 0), (-1, -1), (-1, 1), (1, -1), (1, 1))
MAT = (0, 160, 320, 480, 640, 688, 736, 784)
MROWS = (160,) * 4 + (48,) * 4
HALO = 832
PARTS = (
    (),
    ((0, 72),),
    ((160, 72),),
    ((320, 72),),
    ((480, 72),),
    ((112, 40), (320 + 112, 40), (640, 40)),
    ((160 + 112, 40), (320 + 72, 40), (688, 40)),
    ((72, 40), (480 + 112, 40), (736, 40)),
    ((160 + 72, 40), (480 + 72, 40), (784, 40)),
)
BANDS = 18
FOLD = C // 4
GAINS = 3 * FOLD


def tables():
    def piece(rows, cols, size=None):
        got = [(l * ROWS * COLS + r * COLS + c, r) for l in range(2) for r in rows for c in cols]
        return got + [(-1, None)] * ((size or len(got)) - len(got))

    top, mid, bot = range(0, 3), range(3, 9), range(9, 12)
    left, cen, rig = range(0, 6), range(6, 18), range(18, 24)
    own = [
        piece(mid, cen),
        piece(mid, rig), piece(mid, left), piece(bot, cen), piece(top, cen),
        piece(bot, rig, 40), piece(bot, left, 40), piece(top, rig, 40), piece(top, left, 40),
    ]
    sent = [
        piece(mid, side) + piece(top, side, 40) + piece(bot, side, 48) for side in (left, rig)
    ] + [
        piece(rows, cen) + piece(rows, left, 40) + piece(rows, rig, 48) for rows in (top, bot)
    ] + [
        piece(top, left, 48), piece(top, rig, 48), piece(bot, left, 48), piece(bot, rig, 48),
    ]
    shift = (0, 0, ROWS, -ROWS, ROWS, ROWS, -ROWS, -ROWS)
    flat_own = sum(own, [])
    flat_sent = sum(sent, [])
    moved = sum(
        [[(i, None if r is None else r + s) for i, r in part] for part, s in zip(sent, shift)], []
    )
    assert len(flat_own) == NQS and len(flat_sent) == HALO

    def hot(tokens):
        out = np.zeros((len(tokens), TOK), np.float32)
        for at, (index, _) in enumerate(tokens):
            if index >= 0:
                out[at, index] = 1
        return out

    keys = []
    for w in range(9):
        keys += own[w]
        for start, size in PARTS[w]:
            keys += moved[start : start + size]
    row_of = np.zeros((NKS, 32), np.float32)
    for at, (_, row) in enumerate(keys):
        row_of[at, BANDS if row is None else row + 3] = 1
    to_own, to_sent = hot(flat_own), hot(flat_sent)
    kind = ml_dtypes.bfloat16
    return [
        np.ascontiguousarray(a).astype(kind)
        for a in (np.concatenate([to_own, to_sent]), to_own.T, to_own @ to_sent.T, row_of)
    ]


def dot(a, b, dims=((1,), (0,))):
    return lax.dot_general(a, b, (dims, ((), ())), preferred_element_type=F32)


NT = ((1,), (1,))
TN = ((0,), (0,))


def fold(square):
    return jnp.concatenate([square[FOLD * j : FOLD * (j + 1)] for j in range(4)], 1)


def unfold(wide):
    return jnp.concatenate([wide[:, C * j : C * (j + 1)] for j in range(4)], 0)


def norm(x):
    mean = jnp.mean(x, -1, keepdims=True)
    centred = x - mean
    inverse = lax.rsqrt(jnp.mean(centred * centred, -1, keepdims=True) + 1e-05)
    return centred * inverse, inverse


def norm_back(d, normed, inverse, gain):
    dn = d * gain
    return inverse * (
        dn - jnp.mean(dn, -1, keepdims=True) - normed * jnp.mean(dn * normed, -1, keepdims=True)
    )


class Plan:
    def __init__(self, rows, g1, g2):
        self.r = 16 * -(-rows // (16 * g1))
        self.own = -(-rows // self.r)
        self.rows = self.own * self.r
        self.piece = self.r // 2
        self.across = 3 if g2 >= 6 else 1
        self.pieces = 2 * self.across
        self.lanes = HALF // self.across


def kernel(
    sizes, plans,
    field_in, grad_in, region_in, wqkv_in, wout_in, wup_in, wdown_in, gaina_in, gainm_in,
    gather_in, to_nat_in, collect_in, row_of_in,
    output_hbm, grad_field_hbm, gat_ab_hbm, gat_d_hbm,
    output, grad_field, gat_ab, gat_d,
    field, grad, region, w_qkv, w_out, w_up, w_down, gain_a, gain_m, gather, to_nat, collect, row_of,
    msg, halo_x, back_src, back_dst, back_f,
    x_q, g_q, h1_q, norm_q, norm_h, t_norm, t_win, wpad, qf, kx, vx, closed,
    qm, p0, p1, p2, tile0, tile1, tile2, heads, own_b,
    h2, act, dpre, dmix, dmixb, downs, dq_all, dk_all, dv_all, dsq, out_q,
    ab_src, d_src, ab_rc, d_rc, ab_s0, d_s0, ab_r1, d_r1, ab_s1, d_s1, ab_r2, d_r2,
    ab_fin, d_fin, ab_sh, d_sh,
    in_sem, out_sem, halo_send, halo_recv, core_send, core_recv, red_send, red_recv,
):
    nz, ny, nx, nlat = sizes
    nlon = nz * ny * nx
    g1, g2 = ny * (nlat // 2) * nx, nz
    lon = lax.axis_index("lon")
    lat = lax.axis_index("lat")
    core = lax.rem(lat, 2)
    x_at, y_at, z_at = lax.rem(lon, nx), lax.rem(lax.div(lon, nx), ny), lax.div(lon, nx * ny)
    m1 = (y_at * (nlat // 2) + lax.div(lat, 2)) * nx + x_at
    plan_ab, plan_d = plans

    def wrap(i, n):
        return lax.rem(i + n, n)

    def at(dlat, dlon):
        return {"lon": wrap(lon + dlon, nlon), "lat": wrap(lat + dlat, nlat)}

    def peer1(m):
        y = lax.div(m, nx)
        return {
            "lon": (z_at * ny + lax.div(y, nlat // 2)) * nx + lax.rem(m, nx),
            "lat": lax.rem(y, nlat // 2) * 2 + core,
        }

    def peer2(v):
        return {"lon": v * (nx * ny) + lax.rem(lon, nx * ny), "lat": lat}

    sibling = {"lon": lon, "lat": lat + 1 - 2 * core}

    loads = [
        pltpu.make_async_copy(src, dst, in_sem.at[i])
        for i, (src, dst) in enumerate(
            [
                (field_in, field), (gather_in, gather), (row_of_in, row_of), (gaina_in, gain_a),
                (wqkv_in, w_qkv), (grad_in, grad), (wout_in, w_out), (gainm_in, gain_m),
                (wup_in, w_up), (wdown_in, w_down), (to_nat_in, to_nat), (collect_in, collect),
                (region_in, region),
            ]
        )
    ]
    loads[0].start()
    loads[1].start()
    loads[12].start()
    stores = [
        pltpu.make_async_copy(src, dst, out_sem.at[i])
        for i, (src, dst) in enumerate(
            [
                (output, output_hbm), (grad_field, grad_field_hbm),
                (gat_ab.at[core], gat_ab_hbm.at[core]), (gat_d.at[core], gat_d_hbm.at[core]),
                (gat_ab.at[1 - core], gat_ab_hbm.at[1 - core]),
                (gat_d.at[1 - core], gat_d_hbm.at[1 - core]),
            ]
        )
    ]

    barrier = pltpu.get_barrier_semaphore()

    def greet(device):
        pl.semaphore_signal(barrier, inc=1, device_id=device, device_id_type=MESH)

    def others(n, fn):
        def step(j, _):
            half = lax.div(j, 2)
            fn(n // 2 + jnp.where(lax.rem(j, 2) == 1, half, -half))
            return 0

        lax.fori_loop(1, n, step, 0)

    for way in reversed(WAY):
        greet(at(*way))
    others(g2, lambda k: greet(peer2(wrap(z_at + k, g2))))
    others(g1, lambda k: greet(peer1(wrap(m1 + k, g1))))
    greet(sibling)

    def halo(which, src, dst, sign):
        return [
            pltpu.make_async_remote_copy(
                src_ref=src.at[pl.ds(MAT[i], MROWS[i])],
                dst_ref=dst.at[pl.ds(MAT[i], MROWS[i])],
                send_sem=halo_send.at[which, i],
                recv_sem=halo_recv.at[which, i],
                device_id=at(sign * WAY[i][0], sign * WAY[i][1]),
                device_id_type=MESH,
            )
            for i in range(8)
        ]

    there = halo(0, msg, halo_x, 1)
    back = halo(1, back_src, back_dst, -1)

    lane = lax.broadcasted_iota(jnp.int32, (1, 256), 1)
    for n, tile in ((144, tile0), (72, tile1), (40, tile2)):
        rows = lax.broadcasted_iota(jnp.int32, (n, HEADS * n), 0)
        cols = lax.broadcasted_iota(jnp.int32, (n, HEADS * n), 1)
        hit = jnp.zeros((n, HEADS * n), F32)
        for h in range(HEADS):
            hit = jnp.where(cols == rows + n * h, 1.0, hit)
        tile[...] = hit.astype(BF)
    eye = (
        lax.broadcasted_iota(jnp.int32, (C, C), 0) == lax.broadcasted_iota(jnp.int32, (C, C), 1)
    ).astype(F32).astype(BF)

    loads[0].wait()
    loads[1].wait()
    for load in loads[2:12]:
        load.start()
    msg[...] = dot(gather[NQS:, :], field[...]).astype(BF)
    pl.semaphore_wait(barrier, 9 + (g1 - 1) + (g2 - 1))
    for copy in reversed(there):
        copy.start()
    x_q[...] = dot(gather[0:NQS, :], field[...])

    loads[2].wait()
    loads[12].wait()
    slot = lax.broadcasted_iota(jnp.int32, (32, 256), 0)
    value = jnp.where(slot == BANDS, 3, -1)
    for j in range(BANDS):
        band = region[wrap(lat * ROWS + j - 3, nlat * ROWS)]
        value = jnp.where(slot == j, band, value)
    column = lax.broadcasted_iota(jnp.int32, (32, 256), 1) - C
    band_hot = jnp.where((column >= 0) & (value == column), 1.0, 0.0).astype(BF)
    member = dot(row_of[...], band_hot)
    closed[...] = jnp.where((lane >= C) & (lane < C + 4), (member - 1.0) * 1e30, 0.0)

    for load in loads[3:5]:
        load.wait()
    wpad[...] = jnp.zeros_like(wpad)
    for i in range(3):
        wpad[:, 256 * i : 256 * i + C] = w_qkv[:, C * i : C * i + C]
    gain_attn = gain_a[...]

    normed, inverse1 = norm(x_q[...])
    norm_q[...] = normed
    h1_q[...] = (normed * gain_attn).astype(BF)
    qf[...] = dot(h1_q[...], wpad[:, 0:256]).astype(BF).astype(F32)

    def keys_of(first, last):
        rows = pl.ds(KAT[first], KAT[last] - KAT[first])
        t_win[rows, :] = (t_norm[rows, :] * gain_attn).astype(BF)
        both = dot(t_win[rows, :], wpad[:, 256:768])
        kx[rows, :] = (both[:, 0:256] + member[KAT[first] : KAT[last]]).astype(BF)
        vx[rows, :] = both[:, 256 : 256 + C].astype(BF)

    def kept(w):
        if w == 0:
            return p0, tile0
        return (p1.at[w - 1], tile1) if w < 5 else (p2.at[w - 5], tile2)

    def gather_heads(full, tile):
        n = full.shape[1] // HEADS
        at_lane = lax.broadcasted_iota(jnp.int32, (1, HEADS * n), 1)
        parts = [
            jnp.where(
                (at_lane >= n * h) & (at_lane < n * h + n), full[32 * h : 32 * h + 32], 0.0
            )
            for h in range(HEADS)
        ]
        return dot(tile[...], jnp.concatenate(parts, 0).astype(BF), NT)

    def by_head(inside, outside, width):
        at_lane = lane[:, :width]
        return jnp.concatenate(
            [
                jnp.where((at_lane >= 32 * h) & (at_lane < 32 * h + 32), inside, outside)
                for h in range(HEADS)
            ],
            0,
        ).astype(BF)

    def rows_of(w):
        return pl.ds(QAT[w], NQ[w]), pl.ds(KAT[w], NK[w]), pl.ds(HEADS * QAT[w], HEADS * NQ[w])

    def forward(w):
        q_rows, k_rows, m_rows = rows_of(w)
        keep, tile = kept(w)
        qm[m_rows, :] = by_head(qf[q_rows, :], closed[pl.ds(KAT[w], NQ[w]), :], 256)
        scores = dot(kx[k_rows, :], qm[m_rows, :], NT) * (SCALE * LOG2E)
        top = jnp.max(scores, 0, keepdims=True)
        expo = jnp.exp2(scores - top)
        prob = expo * (1.0 / jnp.sum(expo, 0, keepdims=True))
        keep[...] = prob
        value_t = dot(eye, vx[k_rows, :], NT).astype(BF)
        heads[q_rows, :] = gather_heads(dot(value_t, prob.astype(BF)), tile)

    def backward(w):
        q_rows, k_rows, m_rows = rows_of(w)
        keep, tile = kept(w)
        do = by_head(downs[q_rows, :], 0.0, C)
        prob = keep[...]
        dprob = dot(vx[k_rows, :], do, NT)
        dscore = (prob * (dprob - jnp.sum(dprob * prob, 0, keepdims=True))).astype(BF)
        dv_all[k_rows, :] = dot(prob.astype(BF), do).astype(BF)
        dk_all[k_rows, :] = (dot(dscore, qm[m_rows, 0:C]) * SCALE).astype(BF)
        key_t = dot(eye, kx[k_rows, 0:C], NT).astype(BF)
        dq_all[q_rows, :] = gather_heads(dot(key_t, dscore) * SCALE, tile)

    def mlp(rows):
        x = x_q[rows, :]
        g = g_q[rows, :]
        owned = heads[rows, :].astype(BF)
        own_b[rows, :] = owned
        mixed = x + dot(owned, w_out[...])
        normed2, inverse2 = norm(mixed)
        gain_mlp = gain_m[...]
        h2b = (normed2 * gain_mlp).astype(BF)
        h2[rows, :] = h2b
        pre = dot(h2b, w_up[...])
        square = pre * pre
        tangent = jnp.tanh(0.7978845608 * pre * (1.0 + 0.044715 * square))
        half = 0.5 * (1.0 + tangent)
        actb = (pre * half).astype(BF)
        act[rows, :] = actb
        slope = half + 0.5 * pre * (1.0 - tangent * tangent) * 0.7978845608 * (
            1.0 + 3.0 * 0.044715 * square
        )
        out_q[rows, :] = (mixed + dot(actb, w_down[...], NT)).astype(BF)
        dpreb = (dot(g, w_down[...]) * slope).astype(BF)
        dpre[rows, :] = dpreb
        dh2 = dot(dpreb, w_up[...], NT)
        dm = g.astype(F32) + norm_back(dh2, normed2, inverse2, gain_mlp)
        dmix[rows, :] = dm
        dmb = dm.astype(BF)
        dmixb[rows, :] = dmb
        downs[rows, :] = dot(dmb, w_out[...], NT).astype(BF).astype(F32)
        return jnp.sum(dh2 * normed2, 0, keepdims=True)

    t_norm[0:144, :] = normed[0:144]
    keys_of(0, 1)
    forward(0)
    for load in loads[5:10]:
        load.wait()
    g_q[...] = dot(gather[0:NQS, :], grad[...]).astype(BF)
    term_m = mlp(pl.ds(0, 144))
    backward(0)

    for copy in there:
        copy.wait_recv()
    norm_h[...] = norm(halo_x[...].astype(F32))[0]
    for w in range(1, 9):
        t_norm[pl.ds(KAT[w], NQ[w]), :] = norm_q[pl.ds(QAT[w], NQ[w]), :]
        to = KAT[w] + NQ[w]
        for start, size in PARTS[w]:
            t_norm[pl.ds(to, size), :] = norm_h[pl.ds(start, size), :]
            to += size
    keys_of(1, 9)
    for w in range(1, 9):
        forward(w)
    term_m = term_m + mlp(pl.ds(144, NQS - 144))

    def core_copy(which, stage, src, dst):
        return pltpu.make_async_remote_copy(
            src_ref=src, dst_ref=dst,
            send_sem=core_send.at[which, stage], recv_sem=core_recv.at[which, stage],
            device_id=sibling, device_id_type=MESH,
        )

    def remote(which, stage, k, src, dst, device):
        return pltpu.make_async_remote_copy(
            src_ref=src, dst_ref=dst,
            send_sem=red_send.at[which, stage, k], recv_sem=red_recv.at[which, stage, k],
            device_id=device, device_id_type=MESH,
        )

    def each(n, one, fn, back=None):
        others(n, lambda k: one(k, fn) if back is None else one(k, fn, wrap(back - k, n)))

    def go(copy):
        copy.start()

    def got(copy):
        copy.wait_recv()

    def sent(copy):
        copy.wait_send()

    def split_row(block):
        total = block[0:1] + block[1:2]
        high = total.astype(BF).astype(F32)
        at_row = lax.broadcasted_iota(jnp.int32, block.shape, 0)
        rest = jnp.where(at_row == 1, jnp.broadcast_to(total - high, block.shape), 0.0)
        return jnp.where(at_row == 0, jnp.broadcast_to(high, block.shape), rest).astype(BF)

    class Chain:
        def __init__(self, which, plan, src, rc, s0, r1, s1, r2, fin, sh, gat):
            self.which, self.plan = which, plan
            self.src, self.rc, self.s0, self.r1 = src, rc, s0, r1
            self.s1, self.r2, self.fin, self.sh, self.gat = s1, r2, fin, sh, gat
            self.mine = m1 < plan.own
            self.first = core_copy(which, 0, src.at[1 - core], rc)
            self.last = core_copy(which, 1, gat.at[core], gat.at[core])

        def a2a1(self, k, fn):
            target = wrap(m1 + k, g1)
            start = pl.multiple_of(target * self.plan.r, 16)
            copy = remote(
                self.which, 0, k, self.s0.at[pl.ds(start, self.plan.r)], self.r1.at[k],
                peer1(target),
            )
            pl.when(target < self.plan.own)(functools.partial(fn, copy))

        def come1(self, k, fn):
            fn(remote(self.which, 0, k, self.r1.at[k], self.r1.at[k], peer1(wrap(m1 + k, g1))))

        def a2a2(self, k, fn):
            target = wrap(z_at + k, g2)
            copy = remote(self.which, 1, k, self.s1.at[target], self.r2.at[k], peer2(target))
            pl.when(self.mine & (target < self.plan.pieces))(functools.partial(fn, copy))

        def come2(self, k, fn):
            fn(remote(self.which, 1, k, self.r2.at[k], self.r2.at[k], peer2(wrap(z_at + k, g2))))

        def all2(self, k, fn, source=None):
            source = z_at if source is None else source
            copy = remote(
                self.which, 2, k, self.fin.at[source], self.fin.at[source],
                peer2(wrap(z_at + k, g2)),
            )
            pl.when(self.mine & (source < self.plan.pieces))(functools.partial(fn, copy))

        def all1(self, k, fn, source=None):
            source = m1 if source is None else source
            copy = remote(
                self.which, 3, k, self.sh, self.gat.at[core, source], peer1(wrap(m1 + k, g1))
            )
            pl.when(source < self.plan.own)(functools.partial(fn, copy))

        def begin(self):
            self.first.start()

        def pair(self):
            self.first.wait_recv()
            total = self.src[core] + self.rc[...]
            self.s0[...] = total.astype(BF)
            if self.which == 1:
                self.s0[GAINS : GAINS + 16, :] = split_row(total[GAINS : GAINS + 16])
            each(g1, self.a2a1, go)

        def plane(self):
            plan = self.plan

            @pl.when(self.mine)
            def _():
                each(g1, self.come1, got)
                start = pl.multiple_of(m1 * plan.r, 16)
                total = self.s0[pl.ds(start, plan.r), :].astype(F32)
                for k in range(1, g1):
                    total = total + self.r1[k].astype(F32)
                for j in range(plan.pieces):
                    i, t = j // plan.across, j % plan.across
                    self.s1[j] = total[
                        i * plan.piece : (i + 1) * plan.piece, t * plan.lanes : (t + 1) * plan.lanes
                    ]

            each(g2, self.a2a2, go)

        def line(self):
            @pl.when(self.mine & (z_at < self.plan.pieces))
            def _():
                each(g2, self.come2, got)
                total = self.s1[z_at]
                for k in range(1, g2):
                    total = total + self.r2[k]
                self.fin[z_at] = total

            each(g2, self.all2, go)

        def spread(self):
            each(g2, self.all2, got, z_at)

            @pl.when(self.mine)
            def _():
                across = self.plan.across
                rows = [
                    jnp.concatenate([self.fin[across * i + t] for t in range(across)], 1)
                    for i in range(2)
                ]
                whole = jnp.concatenate(rows, 0)
                shard = whole.astype(BF)
                if self.which == 1:
                    first = jnp.where(m1 == GAINS // self.plan.r, split_row(whole[:16]), shard[:16])
                    shard = first if self.plan.r == 16 else jnp.concatenate([first, shard[16:]], 0)
                self.sh[...] = shard
                self.gat[core, m1] = shard

            each(g1, self.all1, go)

        def collect(self):
            each(g1, self.all1, got, m1)
            self.last.start()

        def end(self):
            self.last.wait_recv()

        def drain(self):
            self.first.wait_send()
            each(g1, self.a2a1, sent)
            each(g2, self.a2a2, sent)

        def drain_late(self):
            each(g2, self.all2, sent)
            each(g1, self.all1, sent)

    ab = Chain(0, plan_ab, ab_src, ab_rc, ab_s0, ab_r1, ab_s1, ab_r2, ab_fin, ab_sh, gat_ab)
    dd = Chain(1, plan_d, d_src, d_rc, d_s0, d_r1, d_s1, d_r2, d_fin, d_sh, gat_d)

    down_term = dot(g_q[...], act[...], TN)
    up_term = dot(h2[...], dpre[...], TN)
    out_term = fold(dot(own_b[...], dmixb[...], TN))
    for i in range(2):
        cols = slice(i * HALF, (i + 1) * HALF)
        ab_src[i, 0:C, :] = down_term[:, cols]
        ab_src[i, C : 2 * C, :] = up_term[:, cols]
        ab_src[i, 2 * C : 2 * C + FOLD, :] = out_term[:, cols]
        if plan_ab.rows > 2 * C + FOLD:
            ab_src[i, 2 * C + FOLD :, :] = jnp.zeros((plan_ab.rows - 2 * C - FOLD, HALF), F32)
    ab.begin()

    for w in range(1, 9):
        backward(w)
        if w == 4:
            ab.pair()

    dsource = dot(dk_all[...], wpad[:, 256 : 256 + C], NT) + dot(dv_all[...], wpad[:, 512 : 512 + C], NT)
    dq_b = dq_all[...].astype(BF)
    dq_source = dot(dq_b, wpad[:, 0:C], NT)
    back_f[...] = jnp.zeros_like(back_f)
    for w in range(9):
        dsq[pl.ds(QAT[w], NQ[w]), :] = (
            dsource[KAT[w] : KAT[w] + NQ[w]] + dq_source[QAT[w] : QAT[w + 1]]
        )
        to = KAT[w] + NQ[w]
        for start, size in PARTS[w]:
            back_f[pl.ds(start, size), :] = dsource[to : to + size]
            to += size
    back_src[...] = back_f[...].astype(BF)
    for copy in reversed(back):
        copy.start()

    term_a = jnp.sum(dsource * t_norm[...], 0, keepdims=True) + jnp.sum(
        dq_source * norm_q[...], 0, keepdims=True
    )
    d_term = jnp.concatenate(
        [
            fold(dot(h1_q[...], dq_b, TN)), fold(dot(t_win[...], dk_all[...], TN)),
            fold(dot(t_win[...], dv_all[...], TN)),
        ],
        0,
    )
    gains = jnp.concatenate([term_a, term_m], 1)
    first_row = lax.broadcasted_iota(jnp.int32, (16, HALF), 0) == 0
    for i in range(2):
        d_src[i, 0:GAINS, :] = d_term[:, i * HALF : (i + 1) * HALF]
        if plan_d.rows > GAINS + 16:
            d_src[i, GAINS + 16 :, :] = jnp.zeros((plan_d.rows - GAINS - 16, HALF), F32)
    d_src[0, GAINS : GAINS + 16, :] = jnp.where(first_row, jnp.broadcast_to(gains, (16, HALF)), 0.0)
    d_src[1, GAINS : GAINS + 16, :] = jnp.zeros((16, HALF), F32)
    dd.begin()

    dd.pair()
    loads[10].wait()
    loads[11].wait()
    output[...] = dot(to_nat[...], out_q[...]).astype(BF)
    stores[0].start()
    ab.plane()
    dd.plane()
    for copy in back:
        copy.wait_recv()
    dshift = (dsq[...] + dot(collect[...], back_dst[...])).astype(BF).astype(F32)
    gf = dmix[...] + norm_back(dshift, norm_q[...], inverse1, gain_attn)
    grad_field[...] = dot(to_nat[...], gf.astype(BF)).astype(BF)
    stores[1].start()
    ab.line()
    dd.line()
    ab.spread()
    dd.spread()
    for copy in there + back:
        copy.wait_send()
    ab.drain()
    dd.drain()
    ab.collect()
    stores[2].start()
    dd.collect()
    stores[3].start()
    ab.drain_late()
    dd.drain_late()
    ab.end()
    stores[4].start()
    dd.end()
    stores[5].start()
    ab.last.wait_send()
    dd.last.wait_send()
    for store in stores:
        store.wait()


def final(plans, out_n, gf_n, gat_ab_in, gat_d_in, *refs):
    outs = refs[:8]
    out_v8, gf_v, gat_ab, gat_d, qkv_v, out_v, up_v, down_v, ga_v, gm_v, in_sem, out_sem = refs[8:]
    loads = [
        pltpu.make_async_copy(src, dst, in_sem.at[i])
        for i, (src, dst) in enumerate(
            [(gat_d_in, gat_d), (gat_ab_in, gat_ab), (out_n, out_v8), (gf_n, gf_v)]
        )
    ]
    for load in loads:
        load.start()
    stores = [
        pltpu.make_async_copy(src, dst, out_sem.at[i])
        for i, (src, dst) in enumerate(
            zip((out_v8, gf_v, qkv_v, out_v, up_v, down_v, ga_v, gm_v), outs)
        )
    ]

    def whole(plan, gat):
        halves = [gat[i].astype(F32).reshape(plan.rows, HALF) for i in range(2)]
        return jnp.concatenate(halves, 1)

    loads[0].wait()
    d = whole(plans[1], gat_d)
    qkv_v[...] = jnp.concatenate([unfold(d[FOLD * i : FOLD * (i + 1)]) for i in range(3)], 1)
    gains = d[GAINS : GAINS + 1] + d[GAINS + 1 : GAINS + 2]
    ga_v[...] = gains[:, :C]
    gm_v[...] = gains[:, C : 2 * C]
    for at in (2, 6, 7):
        stores[at].start()
    for at in range(2):
        loads[2 + at].wait()
        stores[at].start()
    loads[1].wait()
    ab = whole(plans[0], gat_ab)
    down_v[...] = ab[:C]
    up_v[...] = ab[C : 2 * C]
    out_v[...] = unfold(ab[2 * C : 2 * C + FOLD])
    stores[3].start()
    stores[4].start()
    stores[5].start()
    for store in stores:
        store.wait()


def body(nlon, nlat, field, region, w_qkv, w_out, w_up, w_down, gain_attn, gain_mlp, grad_next):
    sizes = (nlon // 8, 2, 4, nlat) if nlon >= 16 else (nlon // 2, 1, 2, nlat)
    nz, ny, nx, _ = sizes
    g1, g2 = ny * (nlat // 2) * nx, nz
    plans = (Plan(2 * C + FOLD, g1, g2), Plan(GAINS + 16, g1, g2))
    hbm = pl.BlockSpec(memory_space=pltpu.HBM)
    V = pltpu.VMEM
    consts = [jnp.asarray(a) for a in tables()]
    operands = [
        field.reshape(TOK, C), grad_next.reshape(TOK, C), region, w_qkv, w_out, w_up, w_down.T,
        gain_attn.reshape(1, C), gain_mlp.reshape(1, C), *consts,
    ]

    def pair(shape_of, kind):
        return [V(shape_of(p), kind) for p in plans]

    shapes = [jax.ShapeDtypeStruct((TOK, C), BF)] * 2 + [
        jax.ShapeDtypeStruct((2, p.own, p.r, HALF), BF) for p in plans
    ]
    scratch = (
        [V(a.shape, a.dtype) for a in shapes]
        + [(pltpu.SMEM if i == 2 else V)(a.shape, a.dtype) for i, a in enumerate(operands)]
        + [V((HALO, C), BF)] * 4 + [V((HALO, C), F32)]
        + [
            V((NQS, C), F32), V((NQS, C), BF), V((NQS, C), BF), V((NQS, C), F32),
            V((HALO, C), F32), V((NKS, C), F32), V((NKS, C), BF), V((C, FF), BF),
            V((NQS, 256), F32), V((NKS, 256), BF), V((NKS, C), BF), V((NKS, 256), F32),
            V((HEADS * NQS, 256), BF),
            V((144, HEADS * 144), F32), V((4, 144, HEADS * 72), F32), V((4, 160, HEADS * 40), F32),
            V((144, HEADS * 144), BF), V((72, HEADS * 72), BF), V((40, HEADS * 40), BF),
            V((NQS, C), F32), V((NQS, C), BF),
            V((NQS, C), BF), V((NQS, FF), BF), V((NQS, FF), BF), V((NQS, C), F32),
            V((NQS, C), BF), V((NQS, C), F32), V((NQS, C), F32),
            V((NKS, C), BF), V((NKS, C), BF), V((NQS, C), F32), V((NQS, C), BF),
        ]
        + pair(lambda p: (2, p.rows, HALF), F32)
        + pair(lambda p: (p.rows, HALF), F32)
        + pair(lambda p: (p.rows, HALF), BF)
        + pair(lambda p: (g1, p.r, HALF), BF)
        + pair(lambda p: (p.pieces, p.piece, p.lanes), F32)
        + pair(lambda p: (g2, p.piece, p.lanes), F32)
        + pair(lambda p: (p.pieces, p.piece, p.lanes), F32)
        + pair(lambda p: (p.r, HALF), BF)
        + [
            pltpu.SemaphoreType.DMA((13,)),
            pltpu.SemaphoreType.DMA((6,)),
            pltpu.SemaphoreType.DMA((2, 8)),
            pltpu.SemaphoreType.DMA((2, 8)),
            pltpu.SemaphoreType.DMA((2, 2)),
            pltpu.SemaphoreType.DMA((2, 2)),
            pltpu.SemaphoreType.DMA((2, 4, 16)),
            pltpu.SemaphoreType.DMA((2, 4, 16)),
        ]
    )
    mids = pl.pallas_call(
        functools.partial(kernel, sizes, plans),
        out_shape=shapes,
        in_specs=[hbm] * len(operands),
        out_specs=[hbm] * 4,
        scratch_shapes=scratch,
        compiler_params=pltpu.CompilerParams(
            collective_id=0, has_side_effects=True, vmem_limit_bytes=VLIM
        ),
        name="block",
    )(*operands)
    results = [
        jax.ShapeDtypeStruct((TOK, C), BF),
        jax.ShapeDtypeStruct((TOK, C), BF),
        jax.ShapeDtypeStruct((C, 3 * C), F32),
        jax.ShapeDtypeStruct((C, C), F32),
        jax.ShapeDtypeStruct((C, FF), F32),
        jax.ShapeDtypeStruct((C, FF), F32),
        jax.ShapeDtypeStruct((1, C), F32),
        jax.ShapeDtypeStruct((1, C), F32),
    ]
    outs = pl.pallas_call(
        functools.partial(final, plans),
        out_shape=results,
        in_specs=[hbm] * 4,
        out_specs=[hbm] * 8,
        scratch_shapes=[V(a.shape, a.dtype) for a in shapes + results[2:]]
        + [pltpu.SemaphoreType.DMA((4,)), pltpu.SemaphoreType.DMA((8,))],
        compiler_params=pltpu.CompilerParams(vmem_limit_bytes=VLIM),
        name="final",
    )(*mids)
    output, grad_field, grad_qkv, grad_out, grad_up, grad_down_t, grad_ga, grad_gm = outs
    return (
        output.reshape(field.shape), grad_field.reshape(field.shape),
        grad_qkv, grad_out, grad_up, grad_down_t.T, grad_ga.reshape(C), grad_gm.reshape(C),
    )


def solution(mesh):
    grid = P(None, "lat", "lon", None)
    return jax.shard_map(
        functools.partial(body, mesh.shape["lon"], mesh.shape["lat"]),
        mesh=mesh,
        in_specs=(grid, P(), P(), P(), P(), P(), P(), P(), grid),
        out_specs=(grid, grid, P(), P(), P(), P(), P(), P()),
        check_vma=False,
    )
```

profile of v0, /device:TPU:1, one launch (start us, length us, event | category | flops | bytes accessed | tf_op | source)
XLA Modules:
  0.0 60.4 jit_solution(1908066485619182186)
XLA Ops:
  0.6 56.9 %block.1 = (bf16[576,192]{1,0:T(8,128)(2,1)}, bf16[576,192]{1,0:T(8,128)(2,1)}, bf16[2,14,32,384]{3,2,1,0:T(8,128)(2,1)}, bf16[2,10,16,384]{3,2,1,0:T(8,128)(2,1)}) custom-call(bf16[576,192]{1,0:T(8,128)(2,1)} %bitcast.10, bf16[576,192]{1,0:T(8,128)(2,1)} %bitcast.11, s32[48]{0:T(128)} %region_in.1, bf16[192,576]{1,0:T(8,128)(2,1)} %wqkv_in.1, ...), custom_call_target="tpu_custom_call" | custom-call | tf_op jit(solution)/shard_map/block/pallas_call | solution.py:750
  57.6 2.7 %final.1 = (bf16[576,192]{1,0:T(8,128)(2,1)}, bf16[576,192]{1,0:T(8,128)(2,1)}, f32[192,576]{1,0:T(8,128)}, f32[192,192]{1,0:T(8,128)}, f32[192,768]{1,0:T(8,128...) custom-call(bf16[576,192]{1,0:T(8,128)(2,1)} %get-tuple-element.20.out_n, ...), custom_call_target="tpu_custom_call" | custom-call | tf_op jit(solution)/shard_map/final/pallas_call | solution.py:771
where the time goes:
time: 60.5 us; the launch traced here: 60.4 us
  Pallas kernels  59.6 us (99%)
  between operations  0.8 us (1%)
    pallas_call x1, Pallas kernels, body(): pl.pallas_call(functools.partial(kernel, sizes, plans), out_shape=shapes,...  56.9 us
    pallas_call x1, Pallas kernels, body(): pl.pallas_call(functools.partial(final, plans), out_shape=results, in_spe...  2.68 us

commit v1 on v0

--- a/solution.py
+++ b/solution.py
@@ -578,19 +578,6 @@
     dsource = dot(dk_all[...], wpad[:, 256 : 256 + C], NT) + dot(dv_all[...], wpad[:, 512 : 512 + C], NT)
     dq_b = dq_all[...].astype(BF)
     dq_source = dot(dq_b, wpad[:, 0:C], NT)
-    back_f[...] = jnp.zeros_like(back_f)
-    for w in range(9):
-        dsq[pl.ds(QAT[w], NQ[w]), :] = (
-            dsource[KAT[w] : KAT[w] + NQ[w]] + dq_source[QAT[w] : QAT[w + 1]]
-        )
-        to = KAT[w] + NQ[w]
-        for start, size in PARTS[w]:
-            back_f[pl.ds(start, size), :] = dsource[to : to + size]
-            to += size
-    back_src[...] = back_f[...].astype(BF)
-    for copy in reversed(back):
-        copy.start()
-
     term_a = jnp.sum(dsource * t_norm[...], 0, keepdims=True) + jnp.sum(
         dq_source * norm_q[...], 0, keepdims=True
     )
@@ -610,6 +597,19 @@
     d_src[0, GAINS : GAINS + 16, :] = jnp.where(first_row, jnp.broadcast_to(gains, (16, HALF)), 0.0)
     d_src[1, GAINS : GAINS + 16, :] = jnp.zeros((16, HALF), F32)
     dd.begin()
+
+    back_f[...] = jnp.zeros_like(back_f)
+    for w in range(9):
+        dsq[pl.ds(QAT[w], NQ[w]), :] = (
+            dsource[KAT[w] : KAT[w] + NQ[w]] + dq_source[QAT[w] : QAT[w + 1]]
+        )
+        to = KAT[w] + NQ[w]
+        for start, size in PARTS[w]:
+            back_f[pl.ds(start, size), :] = dsource[to : to + size]
+            to += size
+    back_src[...] = back_f[...].astype(BF)
+    for copy in reversed(back):
+        copy.start()
 
     dd.pair()
     loads[10].wait()

time: 60.5 us -> 60.7 us (level)
  no operation moved by 1% of the time
where the time goes in v1:
time: 60.7 us; the launch traced here: 60.2 us
  Pallas kernels  59.4 us (98%)
  between operations  0.8 us (1%)
    pallas_call x1, Pallas kernels, body(): pl.pallas_call(functools.partial(kernel, sizes, plans), out_shape=shapes,...  56.7 us
    pallas_call x1, Pallas kernels, body(): pl.pallas_call(functools.partial(final, plans), out_shape=results, in_spe...  2.68 us

profile of v1, /device:TPU:1, one launch (start us, length us, event | category | flops | bytes accessed | tf_op | source)
XLA Modules:
  0.0 60.2 jit_solution(7743961563317440438)
XLA Ops:
  0.6 56.7 %block.1 = (bf16[576,192]{1,0:T(8,128)(2,1)}, bf16[576,192]{1,0:T(8,128)(2,1)}, bf16[2,14,32,384]{3,2,1,0:T(8,128)(2,1)}, bf16[2,10,16,384]{3,2,1,0:T(8,128)(2,1)}) custom-call(bf16[576,192]{1,0:T(8,128)(2,1)} %bitcast.10, bf16[576,192]{1,0:T(8,128)(2,1)} %bitcast.11, s32[48]{0:T(128)} %region_in.1, bf16[192,576]{1,0:T(8,128)(2,1)} %wqkv_in.1, ...), custom_call_target="tpu_custom_call" | custom-call | tf_op jit(solution)/shard_map/block/pallas_call | solution.py:750
  57.4 2.7 %final.1 = (bf16[576,192]{1,0:T(8,128)(2,1)}, bf16[576,192]{1,0:T(8,128)(2,1)}, f32[192,576]{1,0:T(8,128)}, f32[192,192]{1,0:T(8,128)}, f32[192,768]{1,0:T(8,128...) custom-call(bf16[576,192]{1,0:T(8,128)(2,1)} %get-tuple-element.20.out_n, ...), custom_call_target="tpu_custom_call" | custom-call | tf_op jit(solution)/shard_map/final/pallas_call | solution.py:771
